TPU v7x, 32 devices: a whole 2x2x4 slice. The times are simulated.
32 devices in a mesh: groups: 2 (over x), src: 16 (over z, y, core).
Axes of the slice: x: 2, y: 2, z: 4, core: 2. Of those that a mesh axis runs over, the one named last changes fastest.
Arguments:
- waveforms: bfloat16 [2048, 128, 256], P(None, 'src'), may hold values from -0.1875 to 0.1875
- onsets: int32 [4, 128], P('groups', 'src'), parts along dimension 0, may hold values from -256 to 255
- weights: int32 [4, 128], P('groups', 'src'), parts along dimension 0, may hold values from 1 to 13
- active: int32 [4, 128], P('groups', 'src'), parts along dimension 0, may hold values 0 or 1
- rates: bfloat16 [4, 128, 767], P('groups', 'src'), parts along dimension 0, may hold values from 0.099609375 to 2
- gauge_tiles: int32 [32], P('groups'), parts along dimension 0, may hold values from 0 to 15, each once
Outputs:
- forecast: float32 [2048, 4, 512], P('src', 'groups'), parts along dimension 1
There are 2 independent parts, one for each index of `groups`. A program takes and returns all parts, laid end to end along the dimension named above; an argument that names none is the same for every part. Nothing has to cross between parts.
All inputs are finite; a program needn't handle non-finite values. No bound on the sum of `active` on one device may be relied on, other than what follows from the above.
Results may differ from a plain program's by a relative error of at most 0.0028.
Values may be sent and summed in bfloat16 or wider, within the bound.
A program may use at most 128 MiB of HBM per device.

v0:
```python
import functools

import jax
import jax.numpy as jnp
from jax import lax
from jax.experimental import pallas as pl
from jax.experimental.pallas import tpu as pltpu
from jax.sharding import PartitionSpec as P

GTILE = 128
MESH = pl.DeviceIdType.MESH
F32 = jnp.float32
BF16 = jnp.bfloat16


def column(block):
    size = block.shape[1]
    eye = lax.broadcasted_iota(jnp.int32, (size, size), 0) == lax.broadcasted_iota(
        jnp.int32, (size, size), 1
    )
    wide = jnp.broadcast_to(block.astype(F32), (size, size))
    return jnp.sum(jnp.where(eye, wide, 0.0), axis=1, keepdims=True)


def kernel(
    width, scen, samples, taps,
    tiles_ref, onsets_ref, weights_ref, active_ref, rates_ref, w_hbm, out_ref,
    w_ref, scaled, moment, spread, lhs, keep,
    csend, crecv, ysend, yrecv, zsend, zrecv,
    ncs, ncr, nys, nyr, nzs, nzr,
    w_sem, cs_sem, cr_sem, ys_sem, yr_sem, zs_sem, zr_sem, n_ss, n_rs, nz_ss, nz_rs,
):
    line = width // 4
    steps = 2 * line
    rows = out_ref.shape[0]
    local = w_ref.shape[1]
    hist = rates_ref.shape[2]
    columns = scen * samples
    me = lax.axis_index("src")
    z = me // 4
    y = (me // 2) % 2
    core = me % 2
    mate = z * 4 + y * 2 + (1 - core)
    across = z * 4 + (1 - y) * 2 + core

    def peer(j):
        return ((z + 1 + j) % line) * 4 + y * 2 + core

    load = pltpu.make_async_copy(w_hbm, w_ref, w_sem)
    load.start()

    barrier = pltpu.get_barrier_semaphore()
    for other in (mate, across):
        pl.semaphore_signal(barrier, inc=1, device_id={"src": other}, device_id_type=MESH)

    @pl.loop(0, line - 1)
    def _(j):
        pl.semaphore_signal(barrier, inc=1, device_id={"src": peer(j)}, device_id_type=MESH)

    def remote(src, dst, ss, rs, to):
        return pltpu.make_async_remote_copy(
            src_ref=src, dst_ref=dst, send_sem=ss, recv_sem=rs,
            device_id={"src": to}, device_id_type=MESH,
        )

    def ccopy(q):
        return remote(csend.at[q], crecv.at[q], cs_sem.at[q], cr_sem.at[q], mate)

    def ycopy(i):
        return remote(ysend.at[i], yrecv.at[i], ys_sem.at[i], yr_sem.at[i], across)

    def zcopy(j):
        return remote(zsend.at[j], zrecv.at[j], zs_sem.at[j], zr_sem.at[j], peer(j))

    def nzcopy(j):
        return remote(nzs, nzr.at[j], nz_ss.at[j], nz_rs.at[j], peer(j))

    nc = remote(ncs, ncr, n_ss.at[0], n_rs.at[0], mate)
    ny = remote(nys, nyr, n_ss.at[1], n_rs.at[1], across)

    amount = weights_ref[...] * active_ref[...]
    ncs[...] = jnp.broadcast_to(
        jnp.sum((1 + amount).astype(F32), axis=1, keepdims=True), ncs.shape
    )
    scaled[...] = jnp.zeros_like(scaled)
    index = lax.broadcasted_iota(jnp.int32, (local, hist), 1) - (taps - 1)
    for c in range(scen):
        amplitude = column((weights_ref[c : c + 1, :] * active_ref[c : c + 1, :]))
        onset = column(onsets_ref[c : c + 1, :])
        live = index.astype(F32) >= onset
        value = jnp.where(live, amplitude * rates_ref[c].astype(F32), 0.0)
        scaled[c, :, :hist] = value

    padded = scaled.shape[2]
    half = taps // 2

    @pl.loop(0, local)
    def _(s):
        for c in range(scen):
            row = jnp.broadcast_to(scaled[c, pl.ds(s, 1), :], (half, padded))
            turned = pltpu.roll(
                row, shift=padded - (half - 1), axis=1, stride=1, stride_axis=0
            ).astype(BF16)
            base = pl.multiple_of(s * taps, taps)
            where = slice(c * samples, (c + 1) * samples)
            moment[pl.ds(base, half), where] = turned[:, half : half + samples]
            moment[pl.ds(pl.multiple_of(base + half, half), half), where] = turned[:, :samples]

    load.wait()
    pl.semaphore_wait(barrier, 2 + line - 1)
    nc.start()

    def compute(q):
        flip = q // line
        i = q % line
        zz = (z + 1 + i) % line
        yy = (1 - y) * (1 - flip) + y * flip
        for part in range(2):
            cc = (1 - core) * (1 - part) + core * part
            dest = (zz * 4 + yy * 2 + cc) * rows
            gauge = tiles_ref[dest // GTILE] * GTILE + dest % GTILE
            for n in range(taps // 128):
                block = w_ref[pl.ds(gauge, rows), :, n * 128 : (n + 1) * 128]
                spread[n] = block.astype(F32).reshape(rows * local, 128)
            for n in range(taps // 128):
                for s in range(local):
                    lhs[part * rows : (part + 1) * rows, s * taps + n * 128 : s * taps + (n + 1) * 128] = spread[
                        n, pl.ds(s, rows, stride=local), :
                    ].astype(BF16)

        @pl.loop(0, columns // 256)
        def _(n):
            cols = pl.ds(pl.multiple_of(n * 256, 256), 256)
            total = jnp.dot(lhs[...], moment[:, cols], preferred_element_type=F32)
            csend[q, :, cols] = total[:rows].astype(BF16)
            keep[q, :, cols] = total[rows:]

        ccopy(q).start()

    def first(i):
        ccopy(i).wait_recv()
        ysend[i] = (keep[i] + crecv[i].astype(F32)).astype(BF16)
        ycopy(i).start()

        @pl.when(i == 0)
        def _():
            nc.wait()
            nys[...] = ncs[...] + ncr[...]
            ny.start()

    def summed(i):
        ccopy(line + i).wait_recv()
        ycopy(i).wait_recv()
        return keep[line + i] + crecv[line + i].astype(F32) + yrecv[i].astype(F32)

    def second(i):
        zsend[i] = summed(i).astype(BF16)
        zcopy(i).start()

    @pl.loop(0, steps)
    def _(q):
        compute(q)

        @pl.when((q >= 1) & (q <= line))
        def _():
            first(q - 1)

        @pl.when(q == line)
        def _():
            ny.wait()
            nzs[...] = nys[...] + nyr[...]

            @pl.loop(0, line - 1)
            def _(j):
                nzcopy(j).start()

        @pl.when(q >= line + 1)
        def _():
            second(q - line - 1)

    keep[0] = summed(line - 1)

    @pl.loop(0, line - 1)
    def _(j):
        nzcopy(j).wait_recv()
        zcopy(j).wait_recv()

    def add_norm(j, norm):
        return norm + nzr[j]

    norm = lax.fori_loop(0, line - 1, add_norm, nzs[...])
    scale = jnp.full_like(norm, local * width) / norm

    @pl.loop(0, line - 2)
    def _(j):
        keep[0] += zrecv[j].astype(F32)

    for c in range(scen):
        where = slice(c * samples, (c + 1) * samples)
        out_ref[:, where] = (keep[0, :, where] + zrecv[line - 2, :, where].astype(F32)) * scale[
            c : c + 1, :1
        ]

    @pl.loop(0, steps)
    def _(q):
        ccopy(q).wait_send()

    @pl.loop(0, line)
    def _(i):
        ycopy(i).wait_send()

    @pl.loop(0, line - 1)
    def _(j):
        zcopy(j).wait_send()
        nzcopy(j).wait_send()


def per_device(waveforms, onsets, weights, active, rates, gauge_tiles):
    gauges, local, taps = waveforms.shape
    scen, _, hist = rates.shape
    samples = hist - taps + 1
    width = lax.axis_size("src")
    line = width // 4
    rows = gauges // width
    columns = scen * samples
    vmem = pl.BlockSpec(memory_space=pltpu.VMEM)
    dma = pltpu.SemaphoreType.DMA
    out = pl.pallas_call(
        functools.partial(kernel, width, scen, samples, taps),
        out_shape=jax.ShapeDtypeStruct((rows, columns), F32),
        in_specs=[pl.BlockSpec(memory_space=pltpu.SMEM)] + [vmem] * 4 + [pl.BlockSpec(memory_space=pl.ANY)],
        out_specs=vmem,
        scratch_shapes=[
            pltpu.VMEM((gauges, local, taps), BF16),
            pltpu.VMEM((scen, local, hist + 1), F32),
            pltpu.VMEM((local * taps, columns), BF16),
            pltpu.VMEM((taps // 128, rows * local, 128), F32),
            pltpu.VMEM((2 * rows, local * taps), BF16),
            pltpu.VMEM((2 * line, rows, columns), F32),
            pltpu.VMEM((2 * line, rows, columns), BF16),
            pltpu.VMEM((2 * line, rows, columns), BF16),
            pltpu.VMEM((line, rows, columns), BF16),
            pltpu.VMEM((line, rows, columns), BF16),
            pltpu.VMEM((line - 1, rows, columns), BF16),
            pltpu.VMEM((line - 1, rows, columns), BF16),
            pltpu.VMEM((scen, 128), F32),
            pltpu.VMEM((scen, 128), F32),
            pltpu.VMEM((scen, 128), F32),
            pltpu.VMEM((scen, 128), F32),
            pltpu.VMEM((scen, 128), F32),
            pltpu.VMEM((line - 1, scen, 128), F32),
            dma,
            dma((2 * line,)),
            dma((2 * line,)),
            dma((line,)),
            dma((line,)),
            dma((line - 1,)),
            dma((line - 1,)),
            dma((2,)),
            dma((2,)),
            dma((line - 1,)),
            dma((line - 1,)),
        ],
        compiler_params=pltpu.CompilerParams(
            collective_id=0, has_side_effects=True, vmem_limit_bytes=48 * 2**20
        ),
        cost_estimate=pl.CostEstimate(
            flops=2 * gauges * local * taps * columns,
            bytes_accessed=gauges * local * taps * 2,
            transcendentals=0,
        ),
    )(gauge_tiles, onsets, weights, active, rates, waveforms)
    return out.reshape(rows, scen, samples)


def solution(mesh):
    placed = (
        P(None, "src", None),
        P("groups", "src"),
        P("groups", "src"),
        P("groups", "src"),
        P("groups", "src", None),
        P("groups"),
    )
    return jax.shard_map(
        per_device, mesh=mesh, in_specs=placed, out_specs=P("src", "groups", None), check_vma=False
    )
```

profile of v0, /device:TPU:11, one launch (start us, length us, event | category | flops | bytes accessed | tf_op | source)
XLA Modules:
  0.0 50.2 jit_solution(11723239636456507358)
XLA Ops:
  0.0 0.0 copy-start
  0.0 0.7 %copy-done = bf16[2,8,767]{2,1,0:T(8,128)(2,1)S(1)} copy-done((bf16[2,8,767]{2,1,0:T(8,128)(2,1)S(1)}, bf16[2,8,767]{2,1,0:T(8,128)(2,1)}, u32[]{:S(2)}) %copy-start) | copy-done | bytes 24568
  0.7 0.0 copy-start.1
  0.7 0.7 %copy-done.1 = s32[2,8]{1,0:T(2,128)S(1)} copy-done((s32[2,8]{1,0:T(2,128)S(1)}, s32[2,8]{1,0:T(2,128)}, u32[]{:S(2)}) %copy-start.1) | copy-done | bytes 88
  1.4 0.0 copy-start.2
  1.4 0.7 %copy-done.2 = s32[2,8]{1,0:T(2,128)S(1)} copy-done((s32[2,8]{1,0:T(2,128)S(1)}, s32[2,8]{1,0:T(2,128)}, u32[]{:S(2)}) %copy-start.2) | copy-done | bytes 88
  2.1 0.0 copy-start.3
  2.1 0.7 %copy-done.3 = s32[2,8]{1,0:T(2,128)S(1)} copy-done((s32[2,8]{1,0:T(2,128)S(1)}, s32[2,8]{1,0:T(2,128)}, u32[]{:S(2)}) %copy-start.3) | copy-done | bytes 88
  2.8 0.0 copy-start.4
  2.8 0.7 %copy-done.4 = s32[16]{0:T(128)S(1)} copy-done((s32[16]{0:T(128)S(1)}, s32[16]{0:T(128)}, u32[]{:S(2)}) %copy-start.4) | copy-done | bytes 88
  3.4 45.5 %shard_map.64 = f32[128,1024]{1,0:T(8,128)S(1)} custom-call(s32[16]{0:T(128)S(1)} %copy-done.4, s32[2,8]{1,0:T(2,128)S(1)} %copy-done.1, s32[2,8]{1,0:T(2,128)S(1)} %copy-done.2, s32[2,8]{1,0:T(2,128)S(1)} %copy-done.3, bf16[2,8,767]{2,1,0:T(8,128)(2,1)S(1)} %copy-done, bf16[2048,8,256]{2,1,0:T(8,128)(2,1)} %w_hbm.1), custom_call_target="tpu_custom_call" | custom-call | flops 8589934592 | bytes 8388608 | tf_op jit(solution)/shard_map/pallas_call | solution.py:228
  48.9 1.2 %reshape.3 = f32[128,2,512]{2,1,0:T(2,128)} reshape(f32[128,1024]{1,0:T(8,128)S(1)} %shard_map.64) | data formatting | bytes 1048576 | tf_op jit(solution)/shard_map/reshape | solution.py:273
Async XLA Ops:
  0.0 0.7 %copy-start = (bf16[2,8,767]{2,1,0:T(8,128)(2,1)S(1)}, bf16[2,8,767]{2,1,0:T(8,128)(2,1)}, u32[]{:S(2)}) copy-start(bf16[2,8,767]{2,1,0:T(8,128)(2,1)} %rates_ref.1) | copy-start | bytes 73636
  0.7 0.7 %copy-start.1 = (s32[2,8]{1,0:T(2,128)S(1)}, s32[2,8]{1,0:T(2,128)}, u32[]{:S(2)}) copy-start(s32[2,8]{1,0:T(2,128)} %onsets_ref.1) | copy-start | bytes 196
  1.4 0.7 %copy-start.2 = (s32[2,8]{1,0:T(2,128)S(1)}, s32[2,8]{1,0:T(2,128)}, u32[]{:S(2)}) copy-start(s32[2,8]{1,0:T(2,128)} %weights_ref.1) | copy-start | bytes 196
  2.1 0.7 %copy-start.3 = (s32[2,8]{1,0:T(2,128)S(1)}, s32[2,8]{1,0:T(2,128)}, u32[]{:S(2)}) copy-start(s32[2,8]{1,0:T(2,128)} %active_ref.1) | copy-start | bytes 196
  2.8 0.7 %copy-start.4 = (s32[16]{0:T(128)S(1)}, s32[16]{0:T(128)}, u32[]{:S(2)}) copy-start(s32[16]{0:T(128)} %tiles_ref.1) | copy-start | bytes 196
where the time goes:
time: 50.4 us; the launch traced here: 50.2 us
  Pallas kernels  45.5 us (90%)
  local copies, waits for them, and re-layouts  4.66 us (9%)
    pallas_call x1, Pallas kernels, per_device(): pl.pallas_call(functools.partial(kernel, width, scen, samples, taps), out...  45.5 us
    unnamed x10, local copies, waits for them, and re-layouts  3.43 us
    reshape x1, local copies, waits for them, and re-layouts, per_device(): return out.reshape(rows, scen, samples)  1.23 us

commit v1 on v0

--- a/solution.py
+++ b/solution.py
@@ -24,7 +24,8 @@
 
 def kernel(
     width, scen, samples, taps,
-    tiles_ref, onsets_ref, weights_ref, active_ref, rates_ref, w_hbm, out_ref,
+    tiles_hbm, onsets_hbm, weights_hbm, active_hbm, rates_hbm, w_hbm, out_ref,
+    tiles_ref, onsets_ref, weights_ref, active_ref, rates_ref, small_sem,
     w_ref, scaled, moment, spread, lhs, keep,
     csend, crecv, ysend, yrecv, zsend, zrecv,
     ncs, ncr, nys, nyr, nzs, nzr,
@@ -46,6 +47,20 @@
     def peer(j):
         return ((z + 1 + j) % line) * 4 + y * 2 + core
 
+    small = [
+        pltpu.make_async_copy(src, dst, small_sem.at[n])
+        for n, (src, dst) in enumerate(
+            (
+                (rates_hbm, rates_ref),
+                (onsets_hbm, onsets_ref),
+                (weights_hbm, weights_ref),
+                (active_hbm, active_ref),
+                (tiles_hbm, tiles_ref),
+            )
+        )
+    ]
+    for copy in small:
+        copy.start()
     load = pltpu.make_async_copy(w_hbm, w_ref, w_sem)
     load.start()
 
@@ -78,6 +93,8 @@
     nc = remote(ncs, ncr, n_ss.at[0], n_rs.at[0], mate)
     ny = remote(nys, nyr, n_ss.at[1], n_rs.at[1], across)
 
+    for copy in small:
+        copy.wait()
     amount = weights_ref[...] * active_ref[...]
     ncs[...] = jnp.broadcast_to(
         jnp.sum((1 + amount).astype(F32), axis=1, keepdims=True), ncs.shape
@@ -97,9 +114,11 @@
     @pl.loop(0, local)
     def _(s):
         for c in range(scen):
-            row = jnp.broadcast_to(scaled[c, pl.ds(s, 1), :], (half, padded))
-            turned = pltpu.roll(
-                row, shift=padded - (half - 1), axis=1, stride=1, stride_axis=0
+            row = jnp.broadcast_to(scaled[c, pl.ds(s, 1), :], (8, padded))
+            eight = pltpu.roll(row, shift=padded - (half - 1), axis=1, stride=1, stride_axis=0)
+            turned = jnp.concatenate(
+                [eight] + [pltpu.roll(eight, shift=8 * n, axis=1) for n in range(1, half // 8)],
+                axis=0,
             ).astype(BF16)
             base = pl.multiple_of(s * taps, taps)
             where = slice(c * samples, (c + 1) * samples)
@@ -110,9 +129,8 @@
     pl.semaphore_wait(barrier, 2 + line - 1)
     nc.start()
 
-    def compute(q):
-        flip = q // line
-        i = q % line
+    def compute(flip, i):
+        q = flip * line + i
         zz = (z + 1 + i) % line
         yy = (1 - y) * (1 - flip) + y * flip
         for part in range(2):
@@ -140,6 +158,11 @@
     def first(i):
         ccopy(i).wait_recv()
         ysend[i] = (keep[i] + crecv[i].astype(F32)).astype(BF16)
+
+        @pl.when(i > 0)
+        def _():
+            ycopy(i - 1).wait_send()
+
         ycopy(i).start()
 
         @pl.when(i == 0)
@@ -157,15 +180,24 @@
         zsend[i] = summed(i).astype(BF16)
         zcopy(i).start()
 
-    @pl.loop(0, steps)
-    def _(q):
-        compute(q)
-
-        @pl.when((q >= 1) & (q <= line))
-        def _():
-            first(q - 1)
-
-        @pl.when(q == line)
+    @pl.loop(0, steps + 2)
+    def _(p):
+        flip = p % 2
+        i = p // 2 - flip
+
+        @pl.when((i >= 0) & (i < line))
+        def _():
+            compute(flip, i)
+
+        @pl.when((flip == 0) & (i >= 1))
+        def _():
+            first(i - 1)
+
+        @pl.when((flip == 0) & (i >= 2))
+        def _():
+            second(i - 2)
+
+        @pl.when((flip == 0) & (i == 2))
         def _():
             ny.wait()
             nzs[...] = nys[...] + nyr[...]
@@ -173,10 +205,6 @@
             @pl.loop(0, line - 1)
             def _(j):
                 nzcopy(j).start()
-
-        @pl.when(q >= line + 1)
-        def _():
-            second(q - line - 1)
 
     keep[0] = summed(line - 1)
 
@@ -205,9 +233,7 @@
     def _(q):
         ccopy(q).wait_send()
 
-    @pl.loop(0, line)
-    def _(i):
-        ycopy(i).wait_send()
+    ycopy(line - 1).wait_send()
 
     @pl.loop(0, line - 1)
     def _(j):
@@ -228,9 +254,15 @@
     out = pl.pallas_call(
         functools.partial(kernel, width, scen, samples, taps),
         out_shape=jax.ShapeDtypeStruct((rows, columns), F32),
-        in_specs=[pl.BlockSpec(memory_space=pltpu.SMEM)] + [vmem] * 4 + [pl.BlockSpec(memory_space=pl.ANY)],
+        in_specs=[pl.BlockSpec(memory_space=pltpu.HBM)] * 6,
         out_specs=vmem,
         scratch_shapes=[
+            pltpu.SMEM(gauge_tiles.shape, jnp.int32),
+            pltpu.VMEM(onsets.shape, jnp.int32),
+            pltpu.VMEM(weights.shape, jnp.int32),
+            pltpu.VMEM(active.shape, jnp.int32),
+            pltpu.VMEM(rates.shape, BF16),
+            dma((5,)),
             pltpu.VMEM((gauges, local, taps), BF16),
             pltpu.VMEM((scen, local, hist + 1), F32),
             pltpu.VMEM((local * taps, columns), BF16),
@@ -262,7 +294,7 @@
             dma((line - 1,)),
         ],
         compiler_params=pltpu.CompilerParams(
-            collective_id=0, has_side_effects=True, vmem_limit_bytes=48 * 2**20
+            collective_id=0, has_side_effects=True, vmem_limit_bytes=63 * 2**20
         ),
         cost_estimate=pl.CostEstimate(
             flops=2 * gauges * local * taps * columns,

time: 50.4 us -> 45.6 us (0.905)
  local copies, waits for them, and re-layouts: 4.66 us -> 2.27 us
  Pallas kernels: 45.5 us -> 43.2 us
    unnamed x10 -> x0, local copies, waits for them, and re-layouts: 3.43 us -> none
    pallas_call x1, Pallas kernels: 45.5 us -> 43.2 us  [per_device(): pl.pallas_call(functools.partial(kernel, width, scen, samples, taps), out...]
    reshape x1, local copies, waits for them, and re-layouts: 1.23 us -> 2.27 us  [per_device(): return out.reshape(rows, scen, samples)]
where the time goes in v1:
time: 45.6 us; the launch traced here: 45.5 us
  Pallas kernels  43.2 us (95%)
  local copies, waits for them, and re-layouts  2.27 us (5%)
    pallas_call x1, Pallas kernels, per_device(): pl.pallas_call(functools.partial(kernel, width, scen, samples, taps), out...  43.2 us
    reshape x1, local copies, waits for them, and re-layouts, per_device(): return out.reshape(rows, scen, samples)  2.27 us

profile of v1, /device:TPU:11, one launch (start us, length us, event | category | flops | bytes accessed | tf_op | source)
XLA Modules:
  0.0 45.5 jit_solution(9496122282006161090)
XLA Ops:
  0.0 43.2 %shard_map.64 = f32[128,1024]{1,0:T(8,128)} custom-call(s32[16]{0:T(128)} %tiles_hbm.1, s32[2,8]{1,0:T(2,128)} %onsets_hbm.1, s32[2,8]{1,0:T(2,128)} %weights_hbm.1, s32[2,8]{1,0:T(2,128)} %active_hbm.1, bf16[2,8,767]{2,1,0:T(8,128)(2,1)} %rates_hbm.1, bf16[2048,8,256]{2,1,0:T(8,128)(2,1)} %w_hbm.1), custom_call_target="tpu_custom_call" | custom-call | flops 8589934592 | bytes 8388608 | tf_op jit(solution)/shard_map/pallas_call | solution.py:254
  43.2 2.3 %reshape.3 = f32[128,2,512]{2,1,0:T(2,128)} reshape(f32[128,1024]{1,0:T(8,128)} %shard_map.64) | data formatting | bytes 1048576 | tf_op jit(solution)/shard_map/reshape | solution.py:305

commit v2 on v1

--- a/solution.py
+++ b/solution.py
@@ -44,8 +44,12 @@
     mate = z * 4 + y * 2 + (1 - core)
     across = z * 4 + (1 - y) * 2 + core
 
+    def stage(i):
+        ahead = (1 + (i + 1) % (line - 1)) * (1 - i // (line - 1))
+        return (z + ahead) % line
+
     def peer(j):
-        return ((z + 1 + j) % line) * 4 + y * 2 + core
+        return stage(j) * 4 + y * 2 + core
 
     small = [
         pltpu.make_async_copy(src, dst, small_sem.at[n])
@@ -85,7 +89,7 @@
         return remote(ysend.at[i], yrecv.at[i], ys_sem.at[i], yr_sem.at[i], across)
 
     def zcopy(j):
-        return remote(zsend.at[j], zrecv.at[j], zs_sem.at[j], zr_sem.at[j], peer(j))
+        return remote(zsend.at[j], zrecv.at[j], zs_sem.at[j], zr_sem.at[j], peer(j // scen))
 
     def nzcopy(j):
         return remote(nzs, nzr.at[j], nz_ss.at[j], nz_rs.at[j], peer(j))
@@ -131,7 +135,7 @@
 
     def compute(flip, i):
         q = flip * line + i
-        zz = (z + 1 + i) % line
+        zz = stage(i)
         yy = (1 - y) * (1 - flip) + y * flip
         for part in range(2):
             cc = (1 - core) * (1 - part) + core * part
@@ -146,57 +150,67 @@
                         n, pl.ds(s, rows, stride=local), :
                     ].astype(BF16)
 
-        @pl.loop(0, columns // 256)
-        def _(n):
-            cols = pl.ds(pl.multiple_of(n * 256, 256), 256)
-            total = jnp.dot(lhs[...], moment[:, cols], preferred_element_type=F32)
-            csend[q, :, cols] = total[:rows].astype(BF16)
-            keep[q, :, cols] = total[rows:]
-
-        ccopy(q).start()
-
-    def first(i):
-        ccopy(i).wait_recv()
-        ysend[i] = (keep[i] + crecv[i].astype(F32)).astype(BF16)
+        for c in range(scen):
+            k = q * scen + c
+
+            @pl.loop(0, samples // 256)
+            def _(n):
+                cols = pl.ds(pl.multiple_of(n * 256, 256), 256)
+                wide = pl.ds(pl.multiple_of(c * samples + n * 256, 256), 256)
+                total = jnp.dot(lhs[...], moment[:, wide], preferred_element_type=F32)
+                csend[k, :, cols] = total[:rows].astype(BF16)
+                keep[k, :, cols] = total[rows:]
+
+            ccopy(k).start()
+
+    def first(i, c):
+        k = i * scen + c
+        ccopy(k).wait_recv()
+        ysend[k] = (keep[k] + crecv[k].astype(F32)).astype(BF16)
 
         @pl.when(i > 0)
         def _():
-            ycopy(i - 1).wait_send()
-
-        ycopy(i).start()
-
-        @pl.when(i == 0)
+            ycopy(k - scen).wait_send()
+
+        ycopy(k).start()
+
+    def summed(i, c):
+        k = i * scen + c
+        far = line * scen + k
+        ccopy(far).wait_recv()
+        ycopy(k).wait_recv()
+        return keep[far] + crecv[far].astype(F32) + yrecv[k].astype(F32)
+
+    def second(i, c):
+        k = i * scen + c
+        zsend[k] = summed(i, c).astype(BF16)
+        zcopy(k).start()
+
+    @pl.loop(0, steps + 2)
+    def _(p):
+        flip = p % 2
+        i = p // 2 - flip
+
+        @pl.when((i >= 0) & (i < line))
+        def _():
+            compute(flip, i)
+
+        for c in range(scen):
+
+            @pl.when((flip == 0) & (i >= 1))
+            def _():
+                first(i - 1, c)
+
+            @pl.when((flip == 0) & (i >= 2))
+            def _():
+                second(i - 2, c)
+
+        @pl.when((flip == 0) & (i == 1))
         def _():
             nc.wait()
             nys[...] = ncs[...] + ncr[...]
             ny.start()
 
-    def summed(i):
-        ccopy(line + i).wait_recv()
-        ycopy(i).wait_recv()
-        return keep[line + i] + crecv[line + i].astype(F32) + yrecv[i].astype(F32)
-
-    def second(i):
-        zsend[i] = summed(i).astype(BF16)
-        zcopy(i).start()
-
-    @pl.loop(0, steps + 2)
-    def _(p):
-        flip = p % 2
-        i = p // 2 - flip
-
-        @pl.when((i >= 0) & (i < line))
-        def _():
-            compute(flip, i)
-
-        @pl.when((flip == 0) & (i >= 1))
-        def _():
-            first(i - 1)
-
-        @pl.when((flip == 0) & (i >= 2))
-        def _():
-            second(i - 2)
-
         @pl.when((flip == 0) & (i == 2))
         def _():
             ny.wait()
@@ -206,12 +220,12 @@
             def _(j):
                 nzcopy(j).start()
 
-    keep[0] = summed(line - 1)
+    for c in range(scen):
+        keep[c] = summed(line - 1, c)
 
     @pl.loop(0, line - 1)
     def _(j):
         nzcopy(j).wait_recv()
-        zcopy(j).wait_recv()
 
     def add_norm(j, norm):
         return norm + nzr[j]
@@ -221,23 +235,31 @@
 
     @pl.loop(0, line - 2)
     def _(j):
-        keep[0] += zrecv[j].astype(F32)
+        for c in range(scen):
+            k = j * scen + c
+            zcopy(k).wait_recv()
+            keep[c] += zrecv[k].astype(F32)
 
     for c in range(scen):
-        where = slice(c * samples, (c + 1) * samples)
-        out_ref[:, where] = (keep[0, :, where] + zrecv[line - 2, :, where].astype(F32)) * scale[
-            c : c + 1, :1
-        ]
-
-    @pl.loop(0, steps)
+        k = (line - 2) * scen + c
+        zcopy(k).wait_recv()
+        out_ref[:, c * samples : (c + 1) * samples] = (
+            keep[c] + zrecv[k].astype(F32)
+        ) * scale[c : c + 1, :1]
+
+    @pl.loop(0, steps * scen)
     def _(q):
         ccopy(q).wait_send()
 
-    ycopy(line - 1).wait_send()
+    for c in range(scen):
+        ycopy((line - 1) * scen + c).wait_send()
+
+    @pl.loop(0, (line - 1) * scen)
+    def _(k):
+        zcopy(k).wait_send()
 
     @pl.loop(0, line - 1)
     def _(j):
-        zcopy(j).wait_send()
         nzcopy(j).wait_send()
 
 
@@ -253,7 +275,7 @@
     dma = pltpu.SemaphoreType.DMA
     out = pl.pallas_call(
         functools.partial(kernel, width, scen, samples, taps),
-        out_shape=jax.ShapeDtypeStruct((rows, columns), F32),
+        out_shape=pltpu.VMEM((rows, columns), F32),
         in_specs=[pl.BlockSpec(memory_space=pltpu.HBM)] * 6,
         out_specs=vmem,
         scratch_shapes=[
@@ -268,13 +290,13 @@
             pltpu.VMEM((local * taps, columns), BF16),
             pltpu.VMEM((taps // 128, rows * local, 128), F32),
             pltpu.VMEM((2 * rows, local * taps), BF16),
-            pltpu.VMEM((2 * line, rows, columns), F32),
-            pltpu.VMEM((2 * line, rows, columns), BF16),
-            pltpu.VMEM((2 * line, rows, columns), BF16),
-            pltpu.VMEM((line, rows, columns), BF16),
-            pltpu.VMEM((line, rows, columns), BF16),
-            pltpu.VMEM((line - 1, rows, columns), BF16),
-            pltpu.VMEM((line - 1, rows, columns), BF16),
+            pltpu.VMEM((2 * line * scen, rows, samples), F32),
+            pltpu.VMEM((2 * line * scen, rows, samples), BF16),
+            pltpu.VMEM((2 * line * scen, rows, samples), BF16),
+            pltpu.VMEM((line * scen, rows, samples), BF16),
+            pltpu.VMEM((line * scen, rows, samples), BF16),
+            pltpu.VMEM(((line - 1) * scen, rows, samples), BF16),
+            pltpu.VMEM(((line - 1) * scen, rows, samples), BF16),
             pltpu.VMEM((scen, 128), F32),
             pltpu.VMEM((scen, 128), F32),
             pltpu.VMEM((scen, 128), F32),
@@ -282,12 +304,12 @@
             pltpu.VMEM((scen, 128), F32),
             pltpu.VMEM((line - 1, scen, 128), F32),
             dma,
-            dma((2 * line,)),
-            dma((2 * line,)),
-            dma((line,)),
-            dma((line,)),
-            dma((line - 1,)),
-            dma((line - 1,)),
+            dma((2 * line * scen,)),
+            dma((2 * line * scen,)),
+            dma((line * scen,)),
+            dma((line * scen,)),
+            dma(((line - 1) * scen,)),
+            dma(((line - 1) * scen,)),
             dma((2,)),
             dma((2,)),
             dma((line - 1,)),

time: 45.6 us -> 42.1 us (0.923)
  the two profiles are of different devices: /device:TPU:11 before, /device:TPU:0 now
where the time goes in v2:
time: 42.1 us; the launch traced here: 41.9 us
  Pallas kernels  40.7 us (97%)
  local copies, waits for them, and re-layouts  1.23 us (3%)
    pallas_call x1, Pallas kernels, per_device(): pl.pallas_call(functools.partial(kernel, width, scen, samples, taps), out...  40.7 us
    reshape x1, local copies, waits for them, and re-layouts, per_device(): return out.reshape(rows, scen, samples)  1.23 us

profile of v2, /device:TPU:0, one launch (start us, length us, event | category | flops | bytes accessed | tf_op | source)
XLA Modules:
  0.0 41.9 jit_solution(10959106971288361510)
XLA Ops:
  0.0 40.7 %shard_map.64 = f32[128,1024]{1,0:T(8,128)S(1)} custom-call(s32[16]{0:T(128)} %tiles_hbm.1, s32[2,8]{1,0:T(2,128)} %onsets_hbm.1, s32[2,8]{1,0:T(2,128)} %weights_hbm.1, s32[2,8]{1,0:T(2,128)} %active_hbm.1, bf16[2,8,767]{2,1,0:T(8,128)(2,1)} %rates_hbm.1, bf16[2048,8,256]{2,1,0:T(8,128)(2,1)} %w_hbm.1), custom_call_target="tpu_custom_call" | custom-call | flops 8589934592 | bytes 8388608 | tf_op jit(solution)/shard_map/pallas_call | solution.py:276
  40.7 1.2 %reshape.3 = f32[128,2,512]{2,1,0:T(2,128)} reshape(f32[128,1024]{1,0:T(8,128)S(1)} %shard_map.64) | data formatting | bytes 1048576 | tf_op jit(solution)/shard_map/reshape | solution.py:327

commit v3 on v2

--- a/solution.py
+++ b/solution.py
@@ -45,8 +45,12 @@
     across = z * 4 + (1 - y) * 2 + core
 
     def stage(i):
-        ahead = (1 + (i + 1) % (line - 1)) * (1 - i // (line - 1))
-        return (z + ahead) % line
+        pair = (z // 2 + 1 + i // 2) % (line // 2)
+        return pair * 2 + (z + 1 + i) % 2
+
+    def target(i):
+        near = z // 2 * 2 + (z + 1) % 2
+        return (stage(i) * (i % 2) + near * (1 - i % 2)) * 4 + y * 2 + core
 
     def peer(j):
         return stage(j) * 4 + y * 2 + core
@@ -89,7 +93,7 @@
         return remote(ysend.at[i], yrecv.at[i], ys_sem.at[i], yr_sem.at[i], across)
 
     def zcopy(j):
-        return remote(zsend.at[j], zrecv.at[j], zs_sem.at[j], zr_sem.at[j], peer(j // scen))
+        return remote(zsend.at[j], zrecv.at[j], zs_sem.at[j], zr_sem.at[j], target(j // scen))
 
     def nzcopy(j):
         return remote(nzs, nzr.at[j], nz_ss.at[j], nz_rs.at[j], peer(j))
@@ -183,7 +187,16 @@
 
     def second(i, c):
         k = i * scen + c
-        zsend[k] = summed(i, c).astype(BF16)
+
+        @pl.when(i % 2 == 0)
+        def _():
+            zsend[k] = summed(i, c).astype(BF16)
+
+        @pl.when(i % 2 == 1)
+        def _():
+            zcopy(k - scen).wait_recv()
+            zsend[k] = (summed(i, c) + zrecv[k - scen].astype(F32)).astype(BF16)
+
         zcopy(k).start()
 
     @pl.loop(0, steps + 2)
@@ -233,10 +246,10 @@
     norm = lax.fori_loop(0, line - 1, add_norm, nzs[...])
     scale = jnp.full_like(norm, local * width) / norm
 
-    @pl.loop(0, line - 2)
+    @pl.loop(0, line // 2 - 1)
     def _(j):
         for c in range(scen):
-            k = j * scen + c
+            k = (2 * j + 1) * scen + c
             zcopy(k).wait_recv()
             keep[c] += zrecv[k].astype(F32)
 

time: 42.1 us -> 41.2 us (0.979)
  Pallas kernels: 40.7 us -> 39.8 us
    pallas_call x1, Pallas kernels: 40.7 us -> 39.8 us  [per_device(): pl.pallas_call(functools.partial(kernel, width, scen, samples, taps), out...]
where the time goes in v3:
time: 41.2 us; the launch traced here: 41 us
  Pallas kernels  39.8 us (97%)
  local copies, waits for them, and re-layouts  1.23 us (3%)
    pallas_call x1, Pallas kernels, per_device(): pl.pallas_call(functools.partial(kernel, width, scen, samples, taps), out...  39.8 us
    reshape x1, local copies, waits for them, and re-layouts, per_device(): return out.reshape(rows, scen, samples)  1.23 us

profile of v3, /device:TPU:0, one launch (start us, length us, event | category | flops | bytes accessed | tf_op | source)
XLA Modules:
  0.0 41.0 jit_solution(9244246218621532911)
XLA Ops:
  0.0 39.8 %shard_map.64 = f32[128,1024]{1,0:T(8,128)S(1)} custom-call(s32[16]{0:T(128)} %tiles_hbm.1, s32[2,8]{1,0:T(2,128)} %onsets_hbm.1, s32[2,8]{1,0:T(2,128)} %weights_hbm.1, s32[2,8]{1,0:T(2,128)} %active_hbm.1, bf16[2,8,767]{2,1,0:T(8,128)(2,1)} %rates_hbm.1, bf16[2048,8,256]{2,1,0:T(8,128)(2,1)} %w_hbm.1), custom_call_target="tpu_custom_call" | custom-call | flops 8589934592 | bytes 8388608 | tf_op jit(solution)/shard_map/pallas_call | solution.py:289
  39.8 1.2 %reshape.3 = f32[128,2,512]{2,1,0:T(2,128)} reshape(f32[128,1024]{1,0:T(8,128)S(1)} %shard_map.64) | data formatting | bytes 1048576 | tf_op jit(solution)/shard_map/reshape | solution.py:340

commit v4 on v3

--- a/solution.py
+++ b/solution.py
@@ -157,7 +157,7 @@
         for c in range(scen):
             k = q * scen + c
 
-            @pl.loop(0, samples // 256)
+            @pl.loop(0, samples // 256, unroll=True)
             def _(n):
                 cols = pl.ds(pl.multiple_of(n * 256, 256), 256)
                 wide = pl.ds(pl.multiple_of(c * samples + n * 256, 256), 256)

time: 41.2 us -> 40.4 us (0.981)
  Pallas kernels: 39.8 us -> 39 us
    pallas_call x1, Pallas kernels: 39.8 us -> 39 us  [per_device(): pl.pallas_call(functools.partial(kernel, width, scen, samples, taps), out...]
where the time goes in v4:
time: 40.4 us; the launch traced here: 40.3 us
  Pallas kernels  39 us (97%)
  local copies, waits for them, and re-layouts  1.23 us (3%)
    pallas_call x1, Pallas kernels, per_device(): pl.pallas_call(functools.partial(kernel, width, scen, samples, taps), out...  39 us
    reshape x1, local copies, waits for them, and re-layouts, per_device(): return out.reshape(rows, scen, samples)  1.23 us

profile of v4, /device:TPU:0, one launch (start us, length us, event | category | flops | bytes accessed | tf_op | source)
XLA Modules:
  0.0 40.3 jit_solution(8632428269951803712)
XLA Ops:
  0.0 39.0 %shard_map.64 = f32[128,1024]{1,0:T(8,128)S(1)} custom-call(s32[16]{0:T(128)} %tiles_hbm.1, s32[2,8]{1,0:T(2,128)} %onsets_hbm.1, s32[2,8]{1,0:T(2,128)} %weights_hbm.1, s32[2,8]{1,0:T(2,128)} %active_hbm.1, bf16[2,8,767]{2,1,0:T(8,128)(2,1)} %rates_hbm.1, bf16[2048,8,256]{2,1,0:T(8,128)(2,1)} %w_hbm.1), custom_call_target="tpu_custom_call" | custom-call | flops 8589934592 | bytes 8388608 | tf_op jit(solution)/shard_map/pallas_call | solution.py:289
  39.0 1.2 %reshape.3 = f32[128,2,512]{2,1,0:T(2,128)} reshape(f32[128,1024]{1,0:T(8,128)S(1)} %shard_map.64) | data formatting | bytes 1048576 | tf_op jit(solution)/shard_map/reshape | solution.py:340
